TPU v7x, 32 devices: a whole 2x2x4 slice. The times are simulated.
32 devices in a mesh: dom: 8 (over y, x, core), blk: 4 (over z).
Axes of the slice: x: 2, y: 2, z: 4, core: 2. Of those that a mesh axis runs over, the one named last changes fastest.
Arguments:
- features: bfloat16 [32768, 128], P(('dom', 'blk')), may hold values from -6 to 6
- tile_vals: bfloat16 [2304, 128, 128], P(('dom', 'blk')), may hold values from -0.25 to 0.25
- tile_rows: int32 [32, 72], P(('dom', 'blk')), may hold values from 0 to 7
- tile_cols: int32 [32, 72], P(('dom', 'blk')), may hold values from 0 to 7
- tile_count: int32 [32, 4], P(('dom', 'blk')), may hold values from 1 to 18, as said below
- cut_weights: bfloat16 [32768, 384], P(('dom', 'blk')), may hold values from -0.4375 to 0.4375
- send_idx: int32 [32, 384], P(('dom', 'blk')), may hold values from 0 to 1023
- send_count: int32 [32, 8], P(('dom', 'blk')), may hold values from 0 to 48, as said below
- weight: bfloat16 [128, 256], replicated, may hold values from -0.5 to 0.5
- bias: float32 [256], replicated, may hold values from -3 to 3
- cotangent: bfloat16 [32768, 256], P(('dom', 'blk')), may hold values from -6 to 6
Outputs:
- out_y: bfloat16 [32768, 256], P(('dom', 'blk'))
- grad_x: bfloat16 [32768, 128], P(('dom', 'blk'))
- grad_w: float32 [128, 256], replicated
- grad_b: float32 [256], replicated
Inputs may be any that keep to these rules, and one draw needn't show every extreme that they name: `tile_count`: every device has a source position with exactly 18 live slots; devices differ strongly in their counts. `send_count`: zero toward a device's own group; at each index along blk some group receives exactly 48 rows from every other group.
All inputs are finite; a program needn't handle non-finite values.
Results may differ from a plain program's by a relative error of at most 0.018.
Values may be sent and summed in bfloat16 or wider, within the bound.
A program may use at most 128 MiB of HBM per device.

v0:
```python
import math
import jax
import jax.numpy as jnp
from jax import lax
from jax.sharding import PartitionSpec as P


def pad_piece(piece, tile_side):
    padding = jnp.zeros((tile_side, piece.shape[1]), piece.dtype)
    return jnp.concatenate([padding, piece, padding], axis=0)


def pick_blocks(padded, piece_rows, first_rows, tile_side):
    places = jnp.clip(first_rows + tile_side, 0, piece_rows + tile_side)
    picked = jax.vmap(lambda where_at: lax.dynamic_slice_in_dim(padded, where_at, tile_side, 0))(
        places
    )
    inside = (first_rows > -tile_side) & (first_rows < piece_rows)
    return (picked, inside)


def accumulate(running, tiles_here, picked, target, live, flipped):
    row_blocks = running.shape[0]
    selector = (
        (target[:, None] == jnp.arange(row_blocks, dtype=jnp.int32)[None, :]) & live[:, None]
    ).astype(tiles_here.dtype)
    pattern = "tr,tji,tjf->rif" if flipped else "tr,tij,tjf->rif"
    return running + jnp.einsum(
        pattern, selector, tiles_here, picked, preferred_element_type=jnp.float32
    )


def shards(
    features,
    tile_vals,
    tile_rows,
    tile_cols,
    tile_count,
    cut_weights,
    send_idx,
    send_count,
    weight,
    bias,
    cotangent,
):
    rows_dev, feature_width = features.shape
    tile_side = tile_vals.shape[1]
    blk_size = lax.axis_size("blk")
    dom_size = lax.axis_size("dom")
    position = lax.axis_index("blk")
    row_blocks = rows_dev // tile_side
    slot_count = tile_vals.shape[0] // blk_size
    send_most = send_idx.shape[1] // dom_size
    tiles = tile_vals.reshape(blk_size, slot_count, tile_side, tile_side)
    row_ids = tile_rows.reshape(blk_size, slot_count)
    col_ids = tile_cols.reshape(blk_size, slot_count)
    counts = tile_count.reshape(blk_size)
    slot_ids = jnp.arange(slot_count, dtype=jnp.int32)
    live_all = slot_ids[None, :] < counts[:, None]
    sent_rows = send_idx.reshape(dom_size * send_most)
    sent_live = (
        jnp.arange(send_most, dtype=jnp.int32)[None, :] < send_count.reshape(dom_size)[:, None]
    )
    outgoing = jnp.take(features, sent_rows, axis=0).reshape(dom_size, send_most, feature_width)
    outgoing = jnp.where(sent_live[:, :, None], outgoing, jnp.zeros_like(outgoing))
    received = lax.all_to_all(outgoing, "dom", split_axis=0, concat_axis=0, tiled=True)
    cut_part = jnp.dot(
        cut_weights,
        received.reshape(dom_size * send_most, feature_width),
        preferred_element_type=jnp.float32,
    )
    empty = jnp.zeros((row_blocks, tile_side, feature_width), jnp.float32)
    piece = lax.all_gather(features, "blk", axis=0, tiled=True)
    start = jnp.int32(0)
    piece_rows = piece.shape[0]
    padded = pad_piece(piece, tile_side)

    def one_step(source_step, partial_value):
        source = (position - source_step) % blk_size
        lowest = source * rows_dev
        touches = (lowest < start + piece_rows) & (lowest + rows_dev > start)

        def work(inner):
            firsts = lowest + col_ids[source_step] * tile_side
            picked, inside = pick_blocks(padded, piece_rows, firsts, tile_side)
            return accumulate(
                inner,
                tiles[source_step],
                picked,
                row_ids[source_step],
                inside & live_all[source_step],
                False,
            )

        return lax.cond(touches, work, lambda inner: inner, partial_value)

    intra = lax.fori_loop(0, blk_size, one_step, empty).reshape(rows_dev, feature_width)
    aggregated = (intra + cut_part).astype(jnp.bfloat16)
    pre = jnp.dot(aggregated, weight, preferred_element_type=jnp.float32) + bias
    sigmoid_pre = jax.nn.sigmoid(pre)
    out_y = (pre * sigmoid_pre).astype(jnp.bfloat16)
    dpre = (cotangent.astype(jnp.float32) * sigmoid_pre * (1.0 + pre * (1.0 - sigmoid_pre))).astype(
        jnp.bfloat16
    )
    weight_term = lax.dot_general(
        aggregated, dpre, (((0,), (0,)), ((), ())), preferred_element_type=jnp.float32
    )
    bias_term = jnp.sum(dpre.astype(jnp.float32), axis=0)
    dz_rows = lax.dot_general(
        dpre, weight, (((1,), (1,)), ((), ())), preferred_element_type=jnp.float32
    ).astype(jnp.bfloat16)
    cut_back = lax.dot_general(
        cut_weights, dz_rows, (((0,), (0,)), ((), ())), preferred_element_type=jnp.float32
    ).astype(jnp.bfloat16)
    returned = lax.all_to_all(
        cut_back.reshape(dom_size, send_most, feature_width),
        "dom",
        split_axis=0,
        concat_axis=0,
        tiled=True,
    )
    returned = jnp.where(sent_live[:, :, None], returned.astype(jnp.float32), 0.0)
    cut_grad = (
        jnp.zeros((rows_dev, feature_width), jnp.float32)
        .at[sent_rows]
        .add(returned.reshape(dom_size * send_most, feature_width))
    )
    dz_blocks = dz_rows.reshape(row_blocks, tile_side, feature_width)
    row_total = rows_dev * lax.axis_size("blk")

    def one_panel(panel_idx):
        source_step = (position - panel_idx) % blk_size
        picked = jnp.take(dz_blocks, row_ids[source_step], axis=0)
        return accumulate(
            empty, tiles[source_step], picked, col_ids[source_step], live_all[source_step], True
        )

    panel_ids = jnp.arange(row_total // rows_dev, dtype=jnp.int32)
    intra_grad = lax.psum_scatter(
        lax.map(one_panel, panel_ids).reshape(row_total, feature_width),
        "blk",
        scatter_dimension=0,
        tiled=True,
    )
    weight_sum, bias_sum = lax.psum((weight_term, bias_term), ("dom", "blk"))
    scale = 1.0 / math.sqrt(dom_size * blk_size * rows_dev)
    grad_x = (intra_grad + cut_grad).astype(jnp.bfloat16)
    return (out_y, grad_x, weight_sum * scale, bias_sum * scale)


def solution(mesh):
    in_specs = (
        P(("dom", "blk"), None),
        P(("dom", "blk"), None, None),
        P(("dom", "blk"), None),
        P(("dom", "blk"), None),
        P(("dom", "blk"), None),
        P(("dom", "blk"), None),
        P(("dom", "blk"), None),
        P(("dom", "blk"), None),
        P(),
        P(),
        P(("dom", "blk"), None),
    )
    out_specs = (P(("dom", "blk"), None), P(("dom", "blk"), None), P(), P())
    return jax.shard_map(shards, mesh=mesh, in_specs=in_specs, out_specs=out_specs, check_vma=False)
```

profile of v0, /device:TPU:0, one launch (start us, length us, event | category | flops | bytes accessed | tf_op | source)
XLA Modules:
  0.0 325.4 jit_solution(1108997307019440022)
XLA Ops:
  9.4 2.2 gather_fusion.1
  13.1 5.2 %all-to-all-start = ((bf16[8,48,128]{2,1,0:T(8,128)(2,1)}), bf16[8,48,128]{2,1,0:T(8,128)(2,1)S(1)}, u32[]{:S(2)}, u32[]{:S(2)}) async-start(bf16[8,48,128]{2,1,0:T(8,128)(2,1)} %select_select_fusion), calls=%async_computation | async-start | bytes 196608 | tf_op jit(solution)/shard_map/all_to_all | solution.py:66
  22.4 17.8 %all-gather.2.cloned.1.call-done = bf16[4096,128]{1,0:T(8,128)(2,1)} async-done(((bf16[1024,128]{1,0:T(8,128)(2,1)}), bf16[4096,128]{1,0:T(8,128)(2,1)}) %all-gather.2.cloned.1.call-update) | async-done | bytes 1048592 | tf_op jit(solution)/shard_map/all_gather | solution.py:73
  41.6 99.8 %while.34 = (s32[]{:T(128)}, f32[8,128,128]{1,0,2:T(8,128)S(1)}, s32[]{:T(128)}, s32[4,18]{1,0:T(4,128)S(1)}, bf16[4352,128]{1,0:T(8,128)(2,1)S(1)}, /*index=5*/...) while((s32[]{:T(128)}, f32[8,128,128]{1,0,2:T(8,128)S(1)}, ...), condition=%wide.region_3.4_spmd.clone, body=%wide.region_0.3_spmd.clone.sunk | while | flops 80347744 | bytes 3475381 | solution.py:97
  41.7 24.9 %conditional.3 = (f32[8,128,128]{1,0,2:T(8,128)S(1)}) conditional(s32[]{:T(128)} %convert_element_type.66, f32[8,128,128]{1,0,2:T(8,128)S(1)} %get-tuple-element.590, (s32[]{:T(128)}, s32[]{:T(128)}, s32[4,18]{1,0:T(4,128)S(1)}, bf16[4352,128]{1,0:T(8,128)(2,1)S(1)}, bf16[4,18,128,128]{3,2,1,0:T(8,128)(2,1)}, /*index=5*/s32[4,18]{1,0:T(4,128)S(1)}, ...), branch_computations={%region_1.1_spmd, %region_2.2_spmd} | conditional | flops 80347728 | bytes 3474709 | solution.py:95
  41.9 22.6 %while.32 = (s32[]{:T(128)}, bf16[4352,128]{1,0:T(8,128)(2,1)S(1)}, s32[18,2]{0,1:T(2,128)S(1)}, bf16[18,128,128]{2,1,0:T(8,128)(2,1)S(1)}, s32[]{:T(128)}) while((s32[]{:T(128)}, bf16[4352,128]{1,0:T(8,128)(2,1)S(1)}, s32[18,2]{0,1:T(2,128)S(1)}, bf16[18,128,128]{2,1,0:T(8,128)(2,1)S(1)}, s32[]{:T(128)}) %tuple.94), condition=%wide.while_cond, body=%wide.while_body.sunk | while | flops 2 | bytes 65641 | solution.py:15
  64.5 1.6 fusion.10
  66.6 24.9 %conditional.3 = (f32[8,128,128]{1,0,2:T(8,128)S(1)}) conditional(s32[]{:T(128)} %convert_element_type.66, f32[8,128,128]{1,0,2:T(8,128)S(1)} %get-tuple-element.590, (s32[]{:T(128)}, s32[]{:T(128)}, s32[4,18]{1,0:T(4,128)S(1)}, bf16[4352,128]{1,0:T(8,128)(2,1)S(1)}, bf16[4,18,128,128]{3,2,1,0:T(8,128)(2,1)}, /*index=5*/s32[4,18]{1,0:T(4,128)S(1)}, ...), branch_computations={%region_1.1_spmd, %region_2.2_spmd} | conditional | flops 80347728 | bytes 3474709 | solution.py:95
  66.8 22.6 %while.32 = (s32[]{:T(128)}, bf16[4352,128]{1,0:T(8,128)(2,1)S(1)}, s32[18,2]{0,1:T(2,128)S(1)}, bf16[18,128,128]{2,1,0:T(8,128)(2,1)S(1)}, s32[]{:T(128)}) while((s32[]{:T(128)}, bf16[4352,128]{1,0:T(8,128)(2,1)S(1)}, s32[18,2]{0,1:T(2,128)S(1)}, bf16[18,128,128]{2,1,0:T(8,128)(2,1)S(1)}, s32[]{:T(128)}) %tuple.94), condition=%wide.while_cond, body=%wide.while_body.sunk | while | flops 2 | bytes 65641 | solution.py:15
  89.4 1.6 fusion.10
  91.6 24.9 %conditional.3 = (f32[8,128,128]{1,0,2:T(8,128)S(1)}) conditional(s32[]{:T(128)} %convert_element_type.66, f32[8,128,128]{1,0,2:T(8,128)S(1)} %get-tuple-element.590, (s32[]{:T(128)}, s32[]{:T(128)}, s32[4,18]{1,0:T(4,128)S(1)}, bf16[4352,128]{1,0:T(8,128)(2,1)S(1)}, bf16[4,18,128,128]{3,2,1,0:T(8,128)(2,1)}, /*index=5*/s32[4,18]{1,0:T(4,128)S(1)}, ...), branch_computations={%region_1.1_spmd, %region_2.2_spmd} | conditional | flops 80347728 | bytes 3474709 | solution.py:95
  91.7 22.6 %while.32 = (s32[]{:T(128)}, bf16[4352,128]{1,0:T(8,128)(2,1)S(1)}, s32[18,2]{0,1:T(2,128)S(1)}, bf16[18,128,128]{2,1,0:T(8,128)(2,1)S(1)}, s32[]{:T(128)}) while((s32[]{:T(128)}, bf16[4352,128]{1,0:T(8,128)(2,1)S(1)}, s32[18,2]{0,1:T(2,128)S(1)}, bf16[18,128,128]{2,1,0:T(8,128)(2,1)S(1)}, s32[]{:T(128)}) %tuple.94), condition=%wide.while_cond, body=%wide.while_body.sunk | while | flops 2 | bytes 65641 | solution.py:15
  114.4 1.6 fusion.10
  116.5 24.9 %conditional.3 = (f32[8,128,128]{1,0,2:T(8,128)S(1)}) conditional(s32[]{:T(128)} %convert_element_type.66, f32[8,128,128]{1,0,2:T(8,128)S(1)} %get-tuple-element.590, (s32[]{:T(128)}, s32[]{:T(128)}, s32[4,18]{1,0:T(4,128)S(1)}, bf16[4352,128]{1,0:T(8,128)(2,1)S(1)}, bf16[4,18,128,128]{3,2,1,0:T(8,128)(2,1)}, /*index=5*/s32[4,18]{1,0:T(4,128)S(1)}, ...), branch_computations={%region_1.1_spmd, %region_2.2_spmd} | conditional | flops 80347728 | bytes 3474709 | solution.py:95
  116.7 22.6 %while.32 = (s32[]{:T(128)}, bf16[4352,128]{1,0:T(8,128)(2,1)S(1)}, s32[18,2]{0,1:T(2,128)S(1)}, bf16[18,128,128]{2,1,0:T(8,128)(2,1)S(1)}, s32[]{:T(128)}) while((s32[]{:T(128)}, bf16[4352,128]{1,0:T(8,128)(2,1)S(1)}, s32[18,2]{0,1:T(2,128)S(1)}, bf16[18,128,128]{2,1,0:T(8,128)(2,1)S(1)}, s32[]{:T(128)}) %tuple.94), condition=%wide.while_cond, body=%wide.while_body.sunk | while | flops 2 | bytes 65641 | solution.py:15
  139.3 1.6 fusion.10
  141.8 2.5 convert_reduce_fusion
  145.6 20.2 %while.33 = (s32[]{:T(128)}, f32[4,8,128,128]{3,2,1,0:T(8,128)}, s32[4]{0:T(128)S(1)}, s32[]{:T(128)}, s32[4,18]{1,0:T(4,128)S(1)}, /*index=5*/bf16[8,128,128]{2...) while((s32[]{:T(128)}, f32[4,8,128,128]{3,2,1,0:T(8,128)}, ...), condition=%wide.region_5.6_spmd, body=%wide.region_4.5_spmd.sunk | while | flops 80512464 | bytes 6165470 | solution.py:140
  166.9 3.7 %all-to-all-start.1 = ((bf16[8,48,128]{2,1,0:T(8,128)(2,1)}), bf16[8,48,128]{2,1,0:T(8,128)(2,1)S(1)}, u32[]{:S(2)}, u32[]{:S(2)}) async-start(bf16[8,48,128]{2,1,0:T(8,128)(2,1)} %bitcast.26), calls=%async_computation.2 | async-start | bytes 196608 | tf_op jit(solution)/shard_map/all_to_all | solution.py:115
  170.6 40.6 %psum.15 = f32[256]{0:T(256)S(1)} all-reduce(f32[256]{0:T(256)S(1)} %get-tuple-element.426), channel_id=1, replica_groups=mesh['dom'=8,'blk'=4] {'dom','blk'}, use_global_device_ids=true, to_apply=%region_10.11 | all-reduce | flops 256 | bytes 2048 | tf_op jit(solution)/shard_map/psum | solution.py:145
  211.7 56.0 %all-reduce.3.cloned.1.call-done = f32[128,256]{1,0:T(8,128)} async-done(((f32[128,256]{1,0:T(8,128)}), f32[128,256]{1,0:T(8,128)}) %all-reduce.3.cloned.1.call-update) | async-done | bytes 131088 | tf_op jit(solution)/shard_map/psum | solution.py:145
  269.4 43.5 %reduce-scatter.2.cloned.1.call-done = f32[1024,128]{1,0:T(8,128)} async-done(((f32[4096,128]{1,0:T(8,128)}), f32[1024,128]{1,0:T(8,128)}) %reduce-scatter.2.cloned.1.call-update) | async-done | bytes 524304 | tf_op jit(solution)/shard_map/reduce_scatter | solution.py:139
  312.9 4.2 %scatter_fusion = f32[1024,128]{1,0:T(8,128)} fusion(f32[1024,128]{1,0:T(8,128)} %reduce-scatter.2.cloned.1.call-done, s32[384]{0:T(512)S(1)} %fusion.45, f32[384,128]{1,0:T(8,128)S(1)} %bitcast.102), kind=kCustom, calls=%fused_computation.2 | custom fusion | flops 49152 | bytes 591360 | tf_op jit(solution)/shard_map/scatter-add | solution.py:126
  317.1 1.8 convert_element_type.50
  (333 shorter events, 122.7 us)
Async XLA Ops:
  7.2 134.2 %copy-start = (bf16[1024,384]{1,0:T(8,128)(2,1)S(1)}, bf16[1024,384]{1,0:T(8,128)(2,1)}, u32[]{:S(2)}) copy-start(bf16[1024,384]{1,0:T(8,128)(2,1)} %param.22) | copy-start | bytes 2359300
  7.2 33.1 %all-gather.2.cloned.1.call-start = ((), (), s32[]{:S(2)}) async-start(), calls=%async_computation.3 | async-start | bytes 1310720 | tf_op jit(solution)/shard_map/all_gather | solution.py:73
  7.9 33.7 %copy-start.2 = (s32[1,4]{1,0:T(1,128)S(1)}, s32[1,4]{1,0:T(1,128)}, u32[]{:S(2)}) copy-start(s32[1,4]{1,0:T(1,128)} %param.21) | copy-start | bytes 52
  13.1 128.3 %all-to-all-start = ((bf16[8,48,128]{2,1,0:T(8,128)(2,1)}), bf16[8,48,128]{2,1,0:T(8,128)(2,1)S(1)}, u32[]{:S(2)}, u32[]{:S(2)}) async-start(bf16[8,48,128]{2,1,0:T(8,128)(2,1)} %select_select_fusion), calls=%async_computation | async-start | bytes 196608 | tf_op jit(solution)/shard_map/all_to_all | solution.py:66
  18.3 249.4 %all-reduce.3.cloned.1.call-start = ((), (), s32[]{:S(2)}) async-start(), calls=%async_computation.5 | async-start | bytes 262144 | tf_op jit(solution)/shard_map/psum | solution.py:145
  41.6 100.2 %copy-start.1 = (bf16[128,256]{1,0:T(8,128)(2,1)S(1)}, bf16[128,256]{1,0:T(8,128)(2,1)}, u32[]{:S(2)}) copy-start(bf16[128,256]{1,0:T(8,128)(2,1)} %param.25) | copy-start | bytes 196612
  41.6 100.2 %copy-start.3 = (f32[256]{0:T(256)S(1)}, f32[256]{0:T(256)}, u32[]{:S(2)}) copy-start(f32[256]{0:T(256)} %param.26) | copy-start | bytes 3076
  145.6 167.3 %reduce-scatter.2.cloned.1.call-start = ((), (), s32[]{:S(2)}) async-start(), calls=%async_computation.4 | async-start | bytes 2621440 | tf_op jit(solution)/shard_map/reduce_scatter | solution.py:139
  166.9 102.3 %all-to-all-start.1 = ((bf16[8,48,128]{2,1,0:T(8,128)(2,1)}), bf16[8,48,128]{2,1,0:T(8,128)(2,1)S(1)}, u32[]{:S(2)}, u32[]{:S(2)}) async-start(bf16[8,48,128]{2,1,0:T(8,128)(2,1)} %bitcast.26), calls=%async_computation.2 | async-start | bytes 196608 | tf_op jit(solution)/shard_map/all_to_all | solution.py:115
Sparse Core Ops, SparseCore 0:
  9.6 30.6 all-gather.1
  145.7 121.9 all-reduce.2
  270.0 42.8 reduce-scatter.1
where the time goes:
time: 327 us; the launch traced here: 325 us
  waiting for transfers between devices  118 us (36%)
  local copies, waits for them, and re-layouts  102 us (31%)
  blocking collectives  40.6 us (12%)
  matrix products  20.5 us (6%)
  other arithmetic  16.4 us (5%)
  between operations  13.9 us (4%)
  starting transfers between devices  8.96 us (3%)
  loops' own time  4.92 us (2%)
    gather x216, local copies, waits for them, and re-layouts  89 us
    psum x1, waiting for transfers between devices, shards(): weight_sum, bias_sum = lax.psum((weight_term, bias_term), ('dom', 'blk'))  56 us
    reduce_scatter x1, waiting for transfers between devices, shards(): lax.psum_scatter(lax.map(one_panel, panel_ids).reshape(row_total, feature...  43.5 us
    psum x1, blocking collectives, shards(): weight_sum, bias_sum = lax.psum((weight_term, bias_term), ('dom', 'blk'))  40.6 us
    all_gather x1, waiting for transfers between devices, shards(): piece = lax.all_gather(features, 'blk', axis=0, tiled=True)  17.8 us
    dot_general x16, matrix products, accumulate(): jnp.einsum(pattern, selector, tiles_here, picked, preferred_element_type=...  16 us
  transfers between devices with their start and end apart: 5, of which 3 were waited for; matrix products, arithmetic and copies ran while one was open for 40% of the time, Pallas kernels for 0%

commit v1 on v0

--- a/solution.py
+++ b/solution.py
@@ -70,7 +70,21 @@
         preferred_element_type=jnp.float32,
     )
     empty = jnp.zeros((row_blocks, tile_side, feature_width), jnp.float32)
-    piece = lax.all_gather(features, "blk", axis=0, tiled=True)
+    val = lax.axis_index("blk")
+    finding = lax.axis_size("blk")
+    z1, u_next, s_next = (finding, val, features.shape[0])
+    ledger = tuple((jj * z1 if w == 0 else jj for w, jj in enumerate(features.shape)))
+    e_next = jnp.zeros(ledger, features.dtype)
+    f_now = high = features
+    piece = lax.dynamic_update_slice_in_dim(e_next, features, u_next * s_next, axis=0)
+    for u in tuple(range(1, z1 // 2 + 1)):
+        r1 = tuple(((w, (w + 1) % z1) for w in range(z1)))
+        f_now = lax.ppermute(f_now, axis_name="blk", perm=r1)
+        piece = lax.dynamic_update_slice_in_dim(piece, f_now, (u_next - u) % z1 * s_next, axis=0)
+        if 2 * u < z1:
+            low = tuple(((w, (w - 1) % z1) for w in range(z1)))
+            high = lax.ppermute(high, axis_name="blk", perm=low)
+            piece = lax.dynamic_update_slice_in_dim(piece, high, (u_next + u) % z1 * s_next, axis=0)
     start = jnp.int32(0)
     piece_rows = piece.shape[0]
     padded = pad_piece(piece, tile_side)

time: 327 us -> 304 us (0.930)
  waiting for transfers between devices: 118 us -> 83.3 us
  local copies, waits for them, and re-layouts: 102 us -> 108 us
  starting transfers between devices: 8.96 us -> 13.1 us
    reduce_scatter x1, waiting for transfers between devices: 43.5 us -> 0.03 us  [shards(): lax.psum_scatter(lax.map(one_panel, panel_ids).reshape(row_total, feature...]
    psum x1, waiting for transfers between devices: 56 us -> 75.2 us  [shards(): weight_sum, bias_sum = lax.psum((weight_term, bias_term), ('dom', 'blk'))]
    all_gather x1 -> x0, waiting for transfers between devices: 17.8 us -> none  [shards(): piece = lax.all_gather(features, 'blk', axis=0, tiled=True)]
    ppermute x0 -> x3, waiting for transfers between devices: none -> 7.96 us  [the longest x2 7.96 us: shards(): f_now = lax.ppermute(f_now, axis_name='blk', perm=r1)]
    gather x216, local copies, waits for them, and re-layouts: 89 us -> 94.5 us
    ppermute x0 -> x3, starting transfers between devices: none -> 5.17 us  [the longest x2 3.08 us: shards(): f_now = lax.ppermute(f_now, axis_name='blk', perm=r1)]
  transfers between devices with their start and end apart: 5 -> 7, of which waited for: 3 -> 2; matrix products, arithmetic and copies ran while one was open for 40% -> 44% of each run, Pallas kernels for 0% -> 0%
where the time goes in v1:
time: 304 us; the launch traced here: 302 us
  local copies, waits for them, and re-layouts  108 us (36%)
  waiting for transfers between devices  83.3 us (27%)
  blocking collectives  41.8 us (14%)
  matrix products  21.4 us (7%)
  between operations  15.8 us (5%)
  other arithmetic  13.9 us (5%)
  starting transfers between devices  13.1 us (4%)
  loops' own time  4.91 us (2%)
    gather x216, local copies, waits for them, and re-layouts  94.5 us
    psum x1, waiting for transfers between devices, shards(): weight_sum, bias_sum = lax.psum((weight_term, bias_term), ('dom', 'blk'))  75.2 us
    psum x1, blocking collectives, shards(): weight_sum, bias_sum = lax.psum((weight_term, bias_term), ('dom', 'blk'))  41.8 us
    dot_general x16, matrix products, accumulate(): jnp.einsum(pattern, selector, tiles_here, picked, preferred_element_type=...  16.1 us
    ppermute x2, waiting for transfers between devices, shards(): f_now = lax.ppermute(f_now, axis_name='blk', perm=r1)  7.96 us
  transfers between devices with their start and end apart: 7, of which 2 were waited for; matrix products, arithmetic and copies ran while one was open for 44% of the time, Pallas kernels for 0%

profile of v1, /device:TPU:0, one launch (start us, length us, event | category | flops | bytes accessed | tf_op | source)
XLA Modules:
  0.0 302.1 jit_solution(15436064767315982844)
XLA Ops:
  8.0 3.1 %collective-permute-start = (bf16[1024,128]{1,0:T(8,128)(2,1)}, bf16[1024,128]{1,0:T(8,128)(2,1)S(1)}, u32[]{:S(2)}, u32[]{:S(2)}) collective-permute-start(bf16[1024,128]{1,0:T(8,128)(2,1)} %param.17), channel_id=1, source_target_pairs={{0,1},{1,2},{2,3},{3,0},{4,5},{5,6},{6,7},{7,4},{8,9},{9,10},{10,1... | collective-permute-start | bytes 786440 | tf_op jit(solution)/shard_map/ppermute | solution.py:82
  11.1 2.1 collective-permute-start.1
  14.7 2.2 gather_fusion.1
  18.4 4.0 %all-to-all-start = ((bf16[8,48,128]{2,1,0:T(8,128)(2,1)}), bf16[8,48,128]{2,1,0:T(8,128)(2,1)}, u32[]{:S(2)}, u32[]{:S(2)}) async-start(bf16[8,48,128]{2,1,0:T(8,128)(2,1)} %select_select_fusion), calls=%async_computation | async-start | bytes 196608 | tf_op jit(solution)/shard_map/all_to_all | solution.py:66
  25.6 8.0 %collective-permute-done.2 = bf16[1024,128]{1,0:T(8,128)(2,1)S(1)} collective-permute-done((bf16[1024,128]{1,0:T(8,128)(2,1)S(1)}, bf16[1024,128]{1,0:T(8,128)(2,1)S(1)}, u32[]{:S(2)}, u32[]{:S(2)}) %collective-permute-start.2) | collective-permute-done | bytes 262176 | tf_op jit(solution)/shard_map/ppermute | solution.py:82
  33.8 105.3 %while.34 = (s32[]{:T(128)}, f32[8,128,128]{1,0,2:T(8,128)S(1)}, s32[]{:T(128)}, s32[4,18]{1,0:T(4,128)S(1)}, bf16[4352,128]{1,0:T(8,128)(2,1)S(1)}, /*index=5*/...) while((s32[]{:T(128)}, f32[8,128,128]{1,0,2:T(8,128)S(1)}, ...), condition=%wide.region_3.4_spmd.clone, body=%wide.region_0.3_spmd.clone.sunk | while | flops 80347744 | bytes 3475365 | solution.py:111
  33.8 26.3 %conditional.3 = (f32[8,128,128]{1,0,2:T(8,128)S(1)}) conditional(s32[]{:T(128)} %convert_element_type.66, f32[8,128,128]{1,0,2:T(8,128)S(1)} %get-tuple-element.590, (s32[]{:T(128)}, s32[]{:T(128)}, s32[4,18]{1,0:T(4,128)S(1)}, bf16[4352,128]{1,0:T(8,128)(2,1)S(1)}, bf16[4,18,128,128]{3,2,1,0:T(8,128)(2,1)}, /*index=5*/s32[4,18]{1,0:T(4,128)S(1)}, ...), branch_computations={%region_1.1_spmd, %region_2.2_spmd} | conditional | flops 80347728 | bytes 3474701 | solution.py:109
  33.9 24.0 %while.32 = (s32[]{:T(128)}, bf16[4352,128]{1,0:T(8,128)(2,1)S(1)}, s32[18,2]{0,1:T(2,128)S(1)}, bf16[18,128,128]{2,1,0:T(8,128)(2,1)S(1)}, s32[]{:T(128)}) while((s32[]{:T(128)}, bf16[4352,128]{1,0:T(8,128)(2,1)S(1)}, s32[18,2]{0,1:T(2,128)S(1)}, bf16[18,128,128]{2,1,0:T(8,128)(2,1)S(1)}, s32[]{:T(128)}) %tuple.94), condition=%wide.while_cond, body=%wide.while_body.sunk | while | flops 2 | bytes 65633 | solution.py:15
  60.1 26.3 %conditional.3 = (f32[8,128,128]{1,0,2:T(8,128)S(1)}) conditional(s32[]{:T(128)} %convert_element_type.66, f32[8,128,128]{1,0,2:T(8,128)S(1)} %get-tuple-element.590, (s32[]{:T(128)}, s32[]{:T(128)}, s32[4,18]{1,0:T(4,128)S(1)}, bf16[4352,128]{1,0:T(8,128)(2,1)S(1)}, bf16[4,18,128,128]{3,2,1,0:T(8,128)(2,1)}, /*index=5*/s32[4,18]{1,0:T(4,128)S(1)}, ...), branch_computations={%region_1.1_spmd, %region_2.2_spmd} | conditional | flops 80347728 | bytes 3474701 | solution.py:109
  60.2 24.0 %while.32 = (s32[]{:T(128)}, bf16[4352,128]{1,0:T(8,128)(2,1)S(1)}, s32[18,2]{0,1:T(2,128)S(1)}, bf16[18,128,128]{2,1,0:T(8,128)(2,1)S(1)}, s32[]{:T(128)}) while((s32[]{:T(128)}, bf16[4352,128]{1,0:T(8,128)(2,1)S(1)}, s32[18,2]{0,1:T(2,128)S(1)}, bf16[18,128,128]{2,1,0:T(8,128)(2,1)S(1)}, s32[]{:T(128)}) %tuple.94), condition=%wide.while_cond, body=%wide.while_body.sunk | while | flops 2 | bytes 65633 | solution.py:15
  84.2 1.6 fusion.10
  86.4 26.3 %conditional.3 = (f32[8,128,128]{1,0,2:T(8,128)S(1)}) conditional(s32[]{:T(128)} %convert_element_type.66, f32[8,128,128]{1,0,2:T(8,128)S(1)} %get-tuple-element.590, (s32[]{:T(128)}, s32[]{:T(128)}, s32[4,18]{1,0:T(4,128)S(1)}, bf16[4352,128]{1,0:T(8,128)(2,1)S(1)}, bf16[4,18,128,128]{3,2,1,0:T(8,128)(2,1)}, /*index=5*/s32[4,18]{1,0:T(4,128)S(1)}, ...), branch_computations={%region_1.1_spmd, %region_2.2_spmd} | conditional | flops 80347728 | bytes 3474701 | solution.py:109
  86.5 24.0 %while.32 = (s32[]{:T(128)}, bf16[4352,128]{1,0:T(8,128)(2,1)S(1)}, s32[18,2]{0,1:T(2,128)S(1)}, bf16[18,128,128]{2,1,0:T(8,128)(2,1)S(1)}, s32[]{:T(128)}) while((s32[]{:T(128)}, bf16[4352,128]{1,0:T(8,128)(2,1)S(1)}, s32[18,2]{0,1:T(2,128)S(1)}, bf16[18,128,128]{2,1,0:T(8,128)(2,1)S(1)}, s32[]{:T(128)}) %tuple.94), condition=%wide.while_cond, body=%wide.while_body.sunk | while | flops 2 | bytes 65633 | solution.py:15
  110.5 1.6 fusion.10
  112.8 26.3 %conditional.3 = (f32[8,128,128]{1,0,2:T(8,128)S(1)}) conditional(s32[]{:T(128)} %convert_element_type.66, f32[8,128,128]{1,0,2:T(8,128)S(1)} %get-tuple-element.590, (s32[]{:T(128)}, s32[]{:T(128)}, s32[4,18]{1,0:T(4,128)S(1)}, bf16[4352,128]{1,0:T(8,128)(2,1)S(1)}, bf16[4,18,128,128]{3,2,1,0:T(8,128)(2,1)}, /*index=5*/s32[4,18]{1,0:T(4,128)S(1)}, ...), branch_computations={%region_1.1_spmd, %region_2.2_spmd} | conditional | flops 80347728 | bytes 3474701 | solution.py:109
  112.8 24.0 %while.32 = (s32[]{:T(128)}, bf16[4352,128]{1,0:T(8,128)(2,1)S(1)}, s32[18,2]{0,1:T(2,128)S(1)}, bf16[18,128,128]{2,1,0:T(8,128)(2,1)S(1)}, s32[]{:T(128)}) while((s32[]{:T(128)}, bf16[4352,128]{1,0:T(8,128)(2,1)S(1)}, s32[18,2]{0,1:T(2,128)S(1)}, bf16[18,128,128]{2,1,0:T(8,128)(2,1)S(1)}, s32[]{:T(128)}) %tuple.94), condition=%wide.while_cond, body=%wide.while_body.sunk | while | flops 2 | bytes 65633 | solution.py:15
  136.8 1.6 fusion.10
  140.4 2.5 convert_reduce_fusion
  144.2 20.2 %while.33 = (s32[]{:T(128)}, f32[4,8,128,128]{3,2,1,0:T(8,128)}, s32[4]{0:T(128)S(1)}, s32[]{:T(128)}, s32[4,18]{1,0:T(4,128)S(1)}, /*index=5*/bf16[8,128,128]{2...) while((s32[]{:T(128)}, f32[4,8,128,128]{3,2,1,0:T(8,128)}, ...), condition=%wide.region_5.6_spmd, body=%wide.region_4.5_spmd.sunk | while | flops 80512464 | bytes 6165970 | solution.py:154
  165.5 3.9 %all-to-all-start.1 = ((bf16[8,48,128]{2,1,0:T(8,128)(2,1)}), bf16[8,48,128]{2,1,0:T(8,128)(2,1)S(1)}, u32[]{:S(2)}, u32[]{:S(2)}) async-start(bf16[8,48,128]{2,1,0:T(8,128)(2,1)} %bitcast.26), calls=%async_computation.2 | async-start | bytes 196608 | tf_op jit(solution)/shard_map/all_to_all | solution.py:129
  169.3 41.8 %psum.15 = f32[256]{0:T(256)S(1)} all-reduce(f32[256]{0:T(256)S(1)} %get-tuple-element.426), channel_id=1, replica_groups=mesh['dom'=8,'blk'=4] {'dom','blk'}, use_global_device_ids=true, to_apply=%region_10.11 | all-reduce | flops 256 | bytes 2048 | tf_op jit(solution)/shard_map/psum | solution.py:159
  211.7 75.2 %all-reduce.3.cloned.1.call-done = f32[128,256]{1,0:T(8,128)} async-done(((f32[128,256]{1,0:T(8,128)}), f32[128,256]{1,0:T(8,128)}) %all-reduce.3.cloned.1.call-update) | async-done | bytes 131088 | tf_op jit(solution)/shard_map/psum | solution.py:159
  288.7 4.2 %scatter_fusion = f32[1024,128]{1,0:T(8,128)} fusion(f32[1024,128]{1,0:T(8,128)} %reduce-scatter.2.cloned.1.call-done, s32[384]{0:T(512)S(1)} %fusion.45, f32[384,128]{1,0:T(8,128)S(1)} %bitcast.102), kind=kCustom, calls=%fused_computation.2 | custom fusion | flops 49152 | bytes 591360 | tf_op jit(solution)/shard_map/scatter-add | solution.py:140
  292.9 1.8 convert_element_type.50
  (347 shorter events, 127.8 us)
Async XLA Ops:
  8.0 131.1 %copy-start = (bf16[1024,384]{1,0:T(8,128)(2,1)S(1)}, bf16[1024,384]{1,0:T(8,128)(2,1)}, u32[]{:S(2)}) copy-start(bf16[1024,384]{1,0:T(8,128)(2,1)} %param.22) | copy-start | bytes 2359300
  8.0 15.3 %copy-start.1 = (bf16[1024,128]{1,0:T(8,128)(2,1)S(1)}, bf16[1024,128]{1,0:T(8,128)(2,1)}, u32[]{:S(2)}) copy-start(bf16[1024,128]{1,0:T(8,128)(2,1)} %param.17) | copy-start | bytes 786436
  8.0 16.0 %copy-start.5 = (s32[1,72]{1,0:T(1,128)S(1)}, s32[1,72]{1,0:T(1,128)}, u32[]{:S(2)}) copy-start(s32[1,72]{1,0:T(1,128)} %param.20) | copy-start | bytes 868
  8.0 16.7 %copy-start.6 = (s32[1,72]{1,0:T(1,128)S(1)}, s32[1,72]{1,0:T(1,128)}, u32[]{:S(2)}) copy-start(s32[1,72]{1,0:T(1,128)} %param.19) | copy-start | bytes 868
  8.0 15.1 %collective-permute-start = (bf16[1024,128]{1,0:T(8,128)(2,1)}, bf16[1024,128]{1,0:T(8,128)(2,1)S(1)}, u32[]{:S(2)}, u32[]{:S(2)}) collective-permute-start(bf16[1024,128]{1,0:T(8,128)(2,1)} %param.17), channel_id=1, source_target_pairs={{0,1},{1,2},{2,3},{3,0},{4,5},{5,6},{6,7},{7,4},{8,9},{9,10},{10,1... | collective-permute-start | bytes 786440 | tf_op jit(solution)/shard_map/ppermute | solution.py:82
  11.1 14.4 %collective-permute-start.1 = (bf16[1024,128]{1,0:T(8,128)(2,1)}, bf16[1024,128]{1,0:T(8,128)(2,1)S(1)}, u32[]{:S(2)}, u32[]{:S(2)}) collective-permute-start(bf16[1024,128]{1,0:T(8,128)(2,1)} %param.17), channel_id=1, source_target_pairs={{0,3},{1,0},{2,1},{3,2},{4,7},{5,4},{6,5},{7,6},{8,11},{9,8},{10,9... | collective-permute-start | bytes 786440 | tf_op jit(solution)/shard_map/ppermute | solution.py:86
  18.4 120.6 %all-to-all-start = ((bf16[8,48,128]{2,1,0:T(8,128)(2,1)}), bf16[8,48,128]{2,1,0:T(8,128)(2,1)}, u32[]{:S(2)}, u32[]{:S(2)}) async-start(bf16[8,48,128]{2,1,0:T(8,128)(2,1)} %select_select_fusion), calls=%async_computation | async-start | bytes 196608 | tf_op jit(solution)/shard_map/all_to_all | solution.py:66
  22.4 264.6 %all-reduce.3.cloned.1.call-start = ((), (), s32[]{:S(2)}) async-start(), calls=%async_computation.4 | async-start | bytes 262144 | tf_op jit(solution)/shard_map/psum | solution.py:159
  23.2 10.4 %collective-permute-start.2 = (bf16[1024,128]{1,0:T(8,128)(2,1)S(1)}, bf16[1024,128]{1,0:T(8,128)(2,1)S(1)}, u32[]{:S(2)}, u32[]{:S(2)}) collective-permute-start(bf16[1024,128]{1,0:T(8,128)(2,1)S(1)} %collective-permute-done), channel_id=1, source_target_pairs={{0,1},{1,2},{2,3},{3,0},{4,5},{5,6},{6,7},{7,4},{8,9},{9,10},{10,1... | collective-permute-start | bytes 786440 | tf_op jit(solution)/shard_map/ppermute | solution.py:82
  25.5 8.2 %copy-start.3 = (s32[1,4]{1,0:T(1,128)S(1)}, s32[1,4]{1,0:T(1,128)}, u32[]{:S(2)}) copy-start(s32[1,4]{1,0:T(1,128)} %param.21) | copy-start | bytes 52
  33.7 106.6 %copy-start.2 = (bf16[128,256]{1,0:T(8,128)(2,1)S(1)}, bf16[128,256]{1,0:T(8,128)(2,1)}, u32[]{:S(2)}) copy-start(bf16[128,256]{1,0:T(8,128)(2,1)} %param.25) | copy-start | bytes 196612
  33.7 106.6 %copy-start.4 = (f32[256]{0:T(256)S(1)}, f32[256]{0:T(256)}, u32[]{:S(2)}) copy-start(f32[256]{0:T(256)} %param.26) | copy-start | bytes 3076
  144.1 144.6 %reduce-scatter.2.cloned.1.call-start = ((), (), s32[]{:S(2)}) async-start(), calls=%async_computation.3 | async-start | bytes 2621440 | tf_op jit(solution)/shard_map/reduce_scatter | solution.py:153
  165.5 123.1 %all-to-all-start.1 = ((bf16[8,48,128]{2,1,0:T(8,128)(2,1)}), bf16[8,48,128]{2,1,0:T(8,128)(2,1)S(1)}, u32[]{:S(2)}, u32[]{:S(2)}) async-start(bf16[8,48,128]{2,1,0:T(8,128)(2,1)} %bitcast.26), calls=%async_computation.2 | async-start | bytes 196608 | tf_op jit(solution)/shard_map/all_to_all | solution.py:129
Sparse Core Ops, SparseCore 0:
  144.2 142.6 all-reduce.2
Sparse Core Ops, SparseCore 1:
  164.5 43.1 reduce-scatter.1
